TPU v7x, 512 devices: a whole 4x4x16 slice. The times are simulated.
512 devices in a mesh: smp: 128 (over x_lo, z, y), par: 4 (over x_hi, core).
Axes of the slice: x: 4 (x_hi: 2, x_lo: 2; x = x_hi * 2 + x_lo), y: 4, z: 16, core: 2. Of those that a mesh axis runs over, the one named last changes fastest.
Arguments:
- derivatives: bfloat16 [10240, 2048], P('smp', 'par'), may hold values from -40 to 40
- epsilon: float32 [10240], P('smp'), may hold values from -6 to 6
Outputs:
- gram_tile: float32 [10240, 10240], P('smp', 'par')
- update: float32 [2048], P('par')
All inputs are finite; a program needn't handle non-finite values.
Results may differ from a plain program's by a relative error of at most 0.003.
Values may be sent and summed in bfloat16 or wider, within the bound.
A program may use at most 64 MiB of HBM per device.

v0:
```python
import math
import jax
import jax.numpy as jnp
from jax import lax
from jax.sharding import PartitionSpec as P


def shards(derivatives, epsilon):
    total_rows = derivatives.shape[0] * lax.axis_size("smp")
    factor = 1.0 / math.sqrt(total_rows)
    totals = lax.psum(jnp.sum(derivatives.astype(jnp.float32), axis=0), "smp")
    column_mean = totals / total_rows
    own_rows = ((derivatives.astype(jnp.float32) - column_mean) * factor).astype(jnp.bfloat16)
    partial_terms = jnp.dot(
        own_rows,
        lax.all_gather(own_rows, "smp", axis=0, tiled=True).T,
        preferred_element_type=jnp.float32,
    )
    gram_tile = lax.psum_scatter(partial_terms, "par", scatter_dimension=1, tiled=True)
    local_sum = jnp.dot(epsilon, own_rows.astype(jnp.float32), precision=lax.Precision.HIGHEST)
    update = lax.psum(local_sum, "smp")
    return (gram_tile, update)


def solution(mesh):
    in_specs = (P("smp", "par"), P("smp"))
    out_specs = (P("smp", "par"), P("par"))
    return jax.shard_map(shards, mesh=mesh, in_specs=in_specs, out_specs=out_specs, check_vma=False)
```

profile of v0, /device:TPU:4, one launch (start us, length us, event | category | flops | bytes accessed | tf_op | source)
XLA Modules:
  0.0 1246.0 jit_solution(3614393714561013606)
XLA Ops:
  7.2 0.0 copy-start
  7.2 0.0 all-gather.2.cloned.1.call-start
  7.2 0.9 convert_reduce_fusion
  8.1 316.0 %psum.14 = f32[512]{0:T(512)S(1)} all-reduce(f32[512]{0:T(512)S(1)} %convert_reduce_fusion), channel_id=1, replica_groups=mesh['smp'=128,'par'=4] {'smp'}, use_global_device_ids=true, to_apply=%region_1.0 | all-reduce | flops 512 | bytes 4096 | tf_op jit(solution)/shard_map/psum | solution.py:11
  324.1 1.5 fusion.1
  325.7 0.0 copy-start.1
  325.7 0.0 all-gather.2.cloned.1.call-update
  325.7 0.0 reduce-scatter.2.cloned.1.call-start
  325.7 596.6 %all-gather.2.cloned.1.call-done = bf16[10240,512]{1,0:T(8,128)(2,1)} async-done(((bf16[80,512]{1,0:T(8,128)(2,1)}), bf16[10240,512]{1,0:T(8,128)(2,1)}) %all-gather.2.cloned.1.call-update) | async-done | bytes 10485776 | tf_op jit(solution)/shard_map/all_gather | solution.py:16
  922.3 9.1 fusion.4
  931.4 0.0 reduce-scatter.2.cloned.1.call-update
  931.4 0.0 copy-done
  931.4 0.0 copy-done.1
  931.4 0.1 fusion.2
  931.6 307.6 %psum.15 = f32[512]{0:T(512)} all-reduce(f32[512]{0:T(512)S(1)} %bitcast.7), channel_id=1, replica_groups=mesh['smp'=128,'par'=4] {'smp'}, use_global_device_ids=true, to_apply=%region_3.0 | all-reduce | flops 512 | bytes 4096 | tf_op jit(solution)/shard_map/psum | solution.py:21
  1239.2 0.0 reduce-scatter.2.cloned.1.call-done
  (1 shorter events, 0.0 us)
Async XLA Ops:
  7.2 924.2 %copy-start = (f32[80]{0:T(128)S(1)}, f32[80]{0:T(128)}, u32[]{:S(2)}) copy-start(f32[80]{0:T(128)} %param.3) | copy-start | bytes 964
  7.2 915.1 %all-gather.2.cloned.1.call-start = ((), (), s32[]{:S(2)}) async-start(), calls=%async_computation.1 | async-start | bytes 10567680 | tf_op jit(solution)/shard_map/all_gather | solution.py:16
  325.7 605.8 %copy-start.1 = (bf16[80,512]{1,0:T(8,128)(2,1)S(1)}, bf16[80,512]{1,0:T(8,128)(2,1)}, u32[]{:S(2)}) copy-start(bf16[80,512]{1,0:T(8,128)(2,1)} %fusion.1) | copy-start | bytes 245764
  325.7 913.5 %reduce-scatter.2.cloned.1.call-start = ((), (), s32[]{:S(2)}) async-start(), calls=%async_computation.2 | async-start | bytes 4096000 | tf_op jit(solution)/shard_map/reduce_scatter | solution.py:19
Sparse Core Ops, SparseCore 0:
  325.8 596.4 all-gather.1
  931.5 49.1 reduce-scatter.1
where the time goes:
time: 1250 us
  blocking collectives  624 us (50%)
  waiting for transfers between devices  597 us (48%)
  between operations  14.1 us (1%)
    all_gather x1, waiting for transfers between devices, shards(): lax.all_gather(own_rows, 'smp', axis=0, tiled=True)  597 us
    psum x1, blocking collectives, shards(): totals = lax.psum(jnp.sum(derivatives.astype(jnp.float32), axis=0), 'smp')  316 us
    psum x1, blocking collectives, shards(): update = lax.psum(local_sum, 'smp')  308 us
  transfers between devices with their start and end apart: 2, of which 1 were waited for; matrix products, arithmetic and copies ran while one was open for 0% of the time, Pallas kernels for 0%

commit v1 on v0

--- a/solution.py
+++ b/solution.py
@@ -13,7 +13,9 @@
     own_rows = ((derivatives.astype(jnp.float32) - column_mean) * factor).astype(jnp.bfloat16)
     partial_terms = jnp.dot(
         own_rows,
-        lax.all_gather(own_rows, "smp", axis=0, tiled=True).T,
+        jnp.concatenate(
+            lax.all_to_all(jnp.stack([own_rows] * lax.axis_size("smp")), "smp", 0, 0), axis=0
+        ).T,
         preferred_element_type=jnp.float32,
     )
     gram_tile = lax.psum_scatter(partial_terms, "par", scatter_dimension=1, tiled=True)

time: 1250 us -> 1060 us (0.85)
  the two profiles are of different devices: /device:TPU:4 before, /device:TPU:8 now
where the time goes in v1:
time: 1060 us
  blocking collectives  1030 us (97%)
  between operations  14.1 us (1%)
    all_to_all x1, blocking collectives, shards(): lax.all_to_all(jnp.stack([own_rows] * lax.axis_size('smp')), 'smp', 0, 0)  401 us
    psum x1, blocking collectives, shards(): totals = lax.psum(jnp.sum(derivatives.astype(jnp.float32), axis=0), 'smp')  319 us
    psum x1, blocking collectives, shards(): update = lax.psum(local_sum, 'smp')  313 us
  transfers between devices with their start and end apart: 1, of which 0 were waited for; matrix products, arithmetic and copies ran while one was open for 0% of the time, Pallas kernels for 0%

profile of v1, /device:TPU:8, one launch (start us, length us, event | category | flops | bytes accessed | tf_op | source)
XLA Modules:
  0.0 1056.0 jit_solution(15612098877052803742)
XLA Ops:
  7.2 0.0 copy-start
  7.2 0.0 reduce-scatter.2.cloned.1.call-start
  7.2 0.9 convert_reduce_fusion
  8.1 319.4 %psum.14 = f32[512]{0:T(512)S(1)} all-reduce(f32[512]{0:T(512)S(1)} %convert_reduce_fusion), channel_id=1, replica_groups=mesh['smp'=128,'par'=4] {'smp'}, use_global_device_ids=true, to_apply=%region_1.0 | all-reduce | flops 512 | bytes 4096 | tf_op jit(solution)/shard_map/psum | solution.py:11
  327.6 0.9 fusion.1
  328.5 1.3 stack.2
  329.8 400.9 %all_to_all.5 = bf16[128,80,512]{2,1,0:T(8,128)(2,1)S(1)} all-to-all(bf16[128,80,512]{2,1,0:T(8,128)(2,1)S(1)} %stack.2), channel_id=1, replica_groups=mesh['smp'=128,'par'=4] {'smp'}, dimensions={0} | all-to-all | bytes 20971520 | tf_op jit(solution)/shard_map/all_to_all | solution.py:17
  730.7 4.9 fusion.4
  735.7 0.0 reduce-scatter.2.cloned.1.call-update
  735.7 0.0 copy-done
  735.7 0.1 fusion.2
  735.8 313.3 %psum.15 = f32[512]{0:T(512)} all-reduce(f32[512]{0:T(512)S(1)} %bitcast.9), channel_id=1, replica_groups=mesh['smp'=128,'par'=4] {'smp'}, use_global_device_ids=true, to_apply=%region_3.0 | all-reduce | flops 512 | bytes 4096 | tf_op jit(solution)/shard_map/psum | solution.py:23
  1049.1 0.0 reduce-scatter.2.cloned.1.call-done
  (1 shorter events, 0.0 us)
Async XLA Ops:
  7.2 728.5 %copy-start = (f32[80]{0:T(128)S(1)}, f32[80]{0:T(128)}, u32[]{:S(2)}) copy-start(f32[80]{0:T(128)} %param.3) | copy-start | bytes 964
  7.2 1042.0 %reduce-scatter.2.cloned.1.call-start = ((), (), s32[]{:S(2)}) async-start(), calls=%async_computation.2 | async-start | bytes 4096000 | tf_op jit(solution)/shard_map/reduce_scatter | solution.py:21
Sparse Core Ops, SparseCore 0:
  735.8 58.9 reduce-scatter.1
